TPU v7x, 32 devices: a whole 2x2x4 slice. The times are simulated.
32 devices in a mesh: grp: 2 (over y), lon: 16 (over z, x, core).
Axes of the slice: x: 2, y: 2, z: 4, core: 2. Of those that a mesh axis runs over, the one named last changes fastest.
Arguments:
- tokens: bfloat16 [256, 32, 512], P(('grp', 'lon')), parts along dimension 0, may hold values from -30 to 30, as said below
- conv_weight: float32 [3, 3, 512], replicated, may hold values from -1.5 to 1.5
- gain_one: float32 [512], replicated, may hold values from 0.1 to 1.9
- gain_two: float32 [512], replicated, may hold values from 0.1 to 1.9
- w_qkv: bfloat16 [512, 1536], replicated, may hold values from -0.25 to 0.25
- rel_bias: float32 [8, 25, 13], replicated, may hold values from -400 to 400
- w_out: bfloat16 [512, 512], replicated, may hold values from -0.25 to 0.25
- w_up: bfloat16 [512, 2048], replicated, may hold values from -0.25 to 0.25
- w_down: bfloat16 [2048, 512], replicated, may hold values from -0.125 to 0.125
Outputs:
- block_out: bfloat16 [256, 32, 512], P(('grp', 'lon')), parts along dimension 0
There are 2 independent parts, one for each index of `grp`. A program takes and returns all parts, laid end to end along the dimension named above; an argument that names none is the same for every part. Nothing has to cross between parts.
Inputs may be any that keep to these rules, and one draw needn't show every extreme that they name: `tokens`: token features of order one.
All inputs are finite; a program needn't handle non-finite values.
Results may differ from a plain program's by a relative error of at most 0.014.
Values may be sent and summed in bfloat16 or wider, within the bound.
A program may use at most 128 MiB of HBM per device.

v0:
```python
import functools

import jax
import jax.numpy as jnp
from jax import lax
from jax.experimental import pallas as pl
from jax.experimental.pallas import tpu as pltpu
from jax.sharding import PartitionSpec as P

EPS = 1e-05
F32 = jnp.float32
BF16 = jnp.bfloat16
MASKED = -1e30


def norm(values, gain):
    center = values - jnp.mean(values, axis=-1, keepdims=True)
    spread = jnp.mean(center * center, axis=-1, keepdims=True)
    return (center * lax.rsqrt(spread + EPS) * gain).astype(BF16)


def block_kernel(
    dims,
    tok_ref,
    conv_hbm,
    gain_one_hbm,
    gain_two_hbm,
    w_qkv_ref,
    bias_hbm,
    w_out_ref,
    w_up_ref,
    w_down_ref,
    out_ref,
    wide,
    normed,
    mixed,
    q_t,
    k_s,
    v_t,
    att_t,
    bias_s,
    w_qt,
    w_vt,
    score_s,
    prob_s,
    w_qkv,
    w_out,
    w_up,
    w_down,
    conv_ref,
    gain_one_ref,
    gain_two_ref,
    bias_ref,
    load_sem,
    send_sem,
    recv_sem,
):
    columns, lat, width, heads, window, ff = dims
    radius = (window - 1) // 2
    reach = radius + 1
    keys = columns + 2 * radius
    head = width // heads
    tile = 128 // lat
    span = (columns + 2 * radius - tile) * lat
    pairs = heads // 2
    axis = lax.axis_size("lon")
    me = lax.axis_index("lon")
    east, west = lax.rem(me + 1, axis), lax.rem(me + axis - 1, axis)

    barrier = pltpu.get_barrier_semaphore()
    for neighbour in (west, east):
        pl.semaphore_signal(
            barrier, inc=1, device_id={"lon": neighbour}, device_id_type=pl.DeviceIdType.MESH
        )
    loads = [
        pltpu.make_async_copy(tok_ref, wide.at[reach : reach + columns], load_sem.at[0]),
        pltpu.make_async_copy(w_qkv_ref, w_qkv, load_sem.at[1]),
        pltpu.make_async_copy(w_out_ref, w_out, load_sem.at[2]),
        pltpu.make_async_copy(w_up_ref, w_up, load_sem.at[3]),
        pltpu.make_async_copy(w_down_ref, w_down, load_sem.at[4]),
        pltpu.make_async_copy(conv_hbm, conv_ref, load_sem.at[5]),
        pltpu.make_async_copy(gain_one_hbm, gain_one_ref, load_sem.at[6]),
        pltpu.make_async_copy(gain_two_hbm, gain_two_ref, load_sem.at[7]),
        pltpu.make_async_copy(bias_hbm, bias_ref, load_sem.at[8]),
    ]
    for at in (0, 5, 6, 7, 8, 1):
        loads[at].start()
    pl.semaphore_wait(barrier, 2)
    near = 4
    spans = (
        (east, columns - near, reach - near, near),
        (west, 0, reach + columns, near),
        (east, columns - reach, 0, reach - near),
        (west, near, reach + columns + near, reach - near),
    )
    sends = [
        pltpu.make_async_remote_copy(
            src_ref=tok_ref.at[source : source + size],
            dst_ref=wide.at[target : target + size],
            send_sem=send_sem.at[at],
            recv_sem=recv_sem.at[at],
            device_id={"lon": who},
            device_id_type=pl.DeviceIdType.MESH,
        )
        for at, (who, source, target, size) in enumerate(spans)
    ]
    for send in sends:
        send.start()
    for at in (2, 3, 4):
        loads[at].start()
    offsets = 2 * window - 1
    loads[8].wait()
    row = lax.broadcasted_iota(jnp.int32, (128, 128), 0)
    lane = lax.broadcasted_iota(jnp.int32, (128, 128), 1)
    flip = ((lane == (window - 1 - row + 128) % 128) & (row < offsets)).astype(F32)
    turned = []
    for b in range(window):
        piece = jnp.concatenate([bias_ref[b], jnp.zeros((heads, 128 - offsets), F32)], axis=1)
        turned.append(
            jnp.dot(
                piece, flip, preferred_element_type=F32, precision=lax.Precision.HIGHEST
            )
        )
    key_row = lax.broadcasted_iota(jnp.int32, (lat, 128), 0)
    lane = lax.broadcasted_iota(jnp.int32, (lat, 128), 1)
    lane_column = lane // lat
    start = jnp.clip(lane % lat - radius, 0, lat - window)
    inside = (key_row >= start) & (key_row < start + window)
    for kk in range(span // lat):
        line = jnp.zeros((heads, 128), F32)
        for cc in range(tile):
            if 0 <= kk - cc < window:
                line = line + pltpu.roll(turned[kk - cc], cc * lat, 1)
        valid = inside & (lane_column <= kk) & (lane_column > kk - window)
        for h in range(heads):
            spread = jnp.broadcast_to(line[h : h + 1], (lat, 128))
            rolled = pltpu.roll(spread, 0, 1, stride=1, stride_axis=0)
            bias_s[h // 2, kk * lat : (kk + 1) * lat, (h % 2) * 128 : (h % 2 + 1) * 128] = (
                jnp.where(valid, rolled, MASKED)
            )

    rows = lax.broadcasted_iota(jnp.int32, (lat, width), 0)

    def mix(first, count):
        gain_one = gain_one_ref[...]

        def column(index, carry):
            j = first + index
            x = [wide[j + p].astype(F32) for p in range(3)]
            y = [
                conv_ref[0, q : q + 1] * x[0]
                + conv_ref[1, q : q + 1] * x[1]
                + conv_ref[2, q : q + 1] * x[2]
                for q in range(3)
            ]
            above = jnp.where(rows == 0, 0.0, pltpu.roll(y[0], 1, 0))
            below = jnp.where(rows == lat - 1, 0.0, pltpu.roll(y[2], lat - 1, 0))
            total = ((x[1] + y[1]) + (above + below)).astype(BF16)
            mixed[j] = total
            normed[j] = norm(total.astype(F32), gain_one)
            return carry

        lax.fori_loop(0, count, column, 0, unroll=True)

    def project(first, count):
        flat = normed[first : first + count].reshape(count * lat, width)
        at = slice(first * lat, (first + count) * lat)
        k_s[at] = jnp.dot(
            flat, w_qkv[:, width : 2 * width], preferred_element_type=F32
        ).astype(BF16)
        v_t[:, at] = lax.dot_general(
            w_vt[...], flat, (((1,), (1,)), ((), ())), preferred_element_type=F32
        ).astype(BF16)

    for at in (0, 5, 6, 7):
        loads[at].wait()
    mix(reach, columns - 2)
    loads[1].wait()
    w_qt[...] = w_qkv[:, :width].T
    w_vt[...] = w_qkv[:, 2 * width : 3 * width].T
    west_end = -(-reach // tile) * tile
    east_start = (keys - reach) // tile * tile
    project(west_end, east_start - west_end)
    sends[0].wait_recv()
    sends[1].wait_recv()
    mix(reach - near, near)
    mix(reach + columns - 2, near)
    scale = 1.0 / float(head) ** 0.5
    q_t[...] = (
        lax.dot_general(
            w_qt[...],
            normed[radius : radius + columns].reshape(columns * lat, width),
            (((1,), (1,)), ((), ())),
            preferred_element_type=F32,
        ).astype(BF16)
        * scale
    ).astype(BF16)
    project(west_end // 2, west_end // 2)
    project(east_start, tile)
    for at in (2, 3, 4):
        loads[at].wait()
    sends[2].wait_recv()
    sends[3].wait_recv()
    mix(0, reach - near)
    project(0, west_end // 2)
    mix(reach + columns - 2 + near, reach - near)
    project(east_start + tile, keys - east_start - tile)
    blank = jnp.zeros((head, 128), BF16)

    def place(block):
        t, pair = divmod(block, pairs)
        here = slice(t * 128, (t + 1) * 128)
        there = slice(t * 128, t * 128 + span)
        return here, there, pair, slice(pair * 2 * head, (pair + 1) * 2 * head)

    def score(block):
        here, there, pair, at = place(block)
        q_a = q_t[pair * 2 * head : pair * 2 * head + head, here]
        q_b = q_t[pair * 2 * head + head : (pair + 1) * 2 * head, here]
        q_two = jnp.concatenate(
            [jnp.concatenate([q_a, blank], axis=1), jnp.concatenate([blank, q_b], axis=1)],
            axis=0,
        )
        scores = jnp.dot(k_s[there, at], q_two, preferred_element_type=F32) + bias_s[pair]
        score_s[block % 2] = scores
        return jnp.max(scores, axis=0, keepdims=True)

    def soften(block, top):
        expo = jnp.exp(score_s[block % 2] - top)
        prob_s[block % 2] = expo.astype(BF16)
        return jnp.sum(expo, axis=0, keepdims=True)

    def gather(block, denom):
        here, there, pair, at = place(block)
        o = jnp.dot(v_t[at, there], prob_s[block % 2], preferred_element_type=F32)
        o = jnp.concatenate(
            [o[:head, :128] / denom[:, :128], o[head:, 128:] / denom[:, 128:]], axis=0
        )
        att_t[at, here] = o.astype(BF16)

    blocks = columns // tile * pairs
    tops, sums = {}, {}
    for step in range(blocks + 2):
        if step < blocks:
            tops[step] = score(step)
        if 0 <= step - 1 < blocks:
            sums[step - 1] = soften(step - 1, tops[step - 1])
        if 0 <= step - 2 < blocks:
            gather(step - 2, sums[step - 2])

    flat_in = mixed[radius : radius + columns].reshape(columns * lat, width)
    stream = (
        flat_in.astype(F32) + lax.dot_general(
            att_t[...], w_out[...], (((0,), (0,)), ((), ())), preferred_element_type=F32
        )
    ).astype(BF16)
    normed_two = norm(stream.astype(F32), gain_two_ref[...])
    total = stream.astype(F32)
    chunk = 512

    def raise_(at):
        return jnp.dot(normed_two, w_up[:, at : at + chunk], preferred_element_type=F32)

    ahead = raise_(0)
    for at in range(0, ff, chunk):
        now = ahead
        if at + chunk < ff:
            ahead = raise_(at + chunk)
        hidden = jax.nn.gelu(now).astype(BF16)
        total = total + jnp.dot(hidden, w_down[at : at + chunk], preferred_element_type=F32)
    out_ref[...] = total.astype(BF16).reshape(columns, lat, width)
    for send in sends:
        send.wait_send()


def on_device(tokens, conv_weight, gain_one, gain_two, w_qkv, rel_bias, w_out, w_up, w_down):
    columns, lat, width = tokens.shape
    heads, _, window = rel_bias.shape
    ff = w_up.shape[1]
    radius = (window - 1) // 2
    keys = columns + 2 * radius
    dims = (columns, lat, width, heads, window, ff)
    rows = columns * lat
    vmem = pl.BlockSpec(memory_space=pltpu.VMEM)
    hbm = pl.BlockSpec(memory_space=pltpu.MemorySpace.HBM)
    return pl.pallas_call(
        functools.partial(block_kernel, dims),
        out_shape=pltpu.VMEM(tokens.shape, BF16),
        in_specs=[hbm] * 9,
        out_specs=vmem,
        scratch_shapes=[
            pltpu.VMEM((keys + 2, lat, width), BF16),
            pltpu.VMEM((keys, lat, width), BF16),
            pltpu.VMEM((keys, lat, width), BF16),
            pltpu.VMEM((width, rows), BF16),
            pltpu.VMEM((keys * lat, width), BF16),
            pltpu.VMEM((width, keys * lat), BF16),
            pltpu.VMEM((width, rows), BF16),
            pltpu.VMEM((heads // 2, keys * lat - 128, 256), F32),
            pltpu.VMEM((width, width), BF16),
            pltpu.VMEM((width, width), BF16),
            pltpu.VMEM((2, keys * lat - 128, 256), F32),
            pltpu.VMEM((2, keys * lat - 128, 256), BF16),
            pltpu.VMEM(w_qkv.shape, BF16),
            pltpu.VMEM(w_out.shape, BF16),
            pltpu.VMEM(w_up.shape, BF16),
            pltpu.VMEM(w_down.shape, BF16),
            pltpu.VMEM(conv_weight.shape, F32),
            pltpu.VMEM((1, width), F32),
            pltpu.VMEM((1, width), F32),
            pltpu.VMEM((window, heads, rel_bias.shape[1]), F32),
            pltpu.SemaphoreType.DMA((9,)),
            pltpu.SemaphoreType.DMA((4,)),
            pltpu.SemaphoreType.DMA((4,)),
        ],
        compiler_params=pltpu.CompilerParams(
            collective_id=0, has_side_effects=True, vmem_limit_bytes=64 * 1024 * 1024 - 327680
        ),
    )(
        tokens,
        conv_weight,
        gain_one.reshape(1, width),
        gain_two.reshape(1, width),
        w_qkv,
        jnp.transpose(rel_bias, (2, 0, 1)),
        w_out,
        w_up,
        w_down,
    )


def solution(mesh):
    placed = (P(("grp", "lon"), None, None), P(), P(), P(), P(), P(), P(), P(), P())
    return jax.shard_map(
        on_device,
        mesh=mesh,
        in_specs=placed,
        out_specs=P(("grp", "lon"), None, None),
        check_vma=False,
    )
```

profile of v0, /device:TPU:0, one launch (start us, length us, event | category | flops | bytes accessed | tf_op | source)
XLA Modules:
  0.0 15.6 jit_solution(15058507119278954987)
XLA Ops:
  0.0 14.9 %shard_map.91 = bf16[8,32,512]{2,1,0:T(8,128)(2,1)S(1)} custom-call(bf16[8,32,512]{2,1,0:T(8,128)(2,1)} %tok_ref.1, f32[3,3,512]{2,1,0:T(4,128)} %conv_hbm.1, f32[1,512]{1,0:T(1,128)} %bitcast.4, f32[1,512]{1,0:T(1,128)} %bitcast.5, bf16[512,1536]{1,0:T(8,128)(2,1)} %w_qkv_ref.1, f32[13,8,25]{2,1,0:T(8,128)} %bitcast.3, bf16[512,512]{1,0:T(8,128)(2,1)} %w_out_ref.1, ...), custom_call_target="tpu_custom_call" | custom-call | tf_op jit(solution)/shard_map/pallas_call | solution.py:286
  14.9 0.7 %copy.11 = bf16[8,32,512]{2,1,0:T(8,128)(2,1)} copy(bf16[8,32,512]{2,1,0:T(8,128)(2,1)S(1)} %shard_map.91) | data formatting | bytes 524288
where the time goes:
time: 15.8 us; the launch traced here: 15.6 us
  Pallas kernels  14.9 us (94%)
  local copies, waits for them, and re-layouts  0.71 us (4%)
    pallas_call x1, Pallas kernels, on_device(): pl.pallas_call(functools.partial(block_kernel, dims), out_shape=pltpu.VME...  14.9 us
    unnamed x1, local copies, waits for them, and re-layouts  0.71 us

commit v1 on v0

--- a/solution.py
+++ b/solution.py
@@ -17,6 +17,12 @@
     center = values - jnp.mean(values, axis=-1, keepdims=True)
     spread = jnp.mean(center * center, axis=-1, keepdims=True)
     return (center * lax.rsqrt(spread + EPS) * gain).astype(BF16)
+
+
+def gelu(x):
+    half = x * BF16(0.5)
+    inner = x * (BF16(0.7978845608028654) + BF16(0.035677408136300125) * (x * x))
+    return half + half * jnp.tanh(inner)
 
 
 def block_kernel(
@@ -43,6 +49,9 @@
     w_vt,
     score_s,
     prob_s,
+    top_s,
+    sum_s,
+    held,
     w_qkv,
     w_out,
     w_up,
@@ -63,9 +72,13 @@
     tile = 128 // lat
     span = (columns + 2 * radius - tile) * lat
     pairs = heads // 2
+    near = reach - tile
+    groups = keys // tile
     axis = lax.axis_size("lon")
     me = lax.axis_index("lon")
     east, west = lax.rem(me + 1, axis), lax.rem(me + axis - 1, axis)
+    core = lax.rem(me, 2)
+    odd = jnp.where(me == 1, 0, core)
 
     barrier = pltpu.get_barrier_semaphore()
     for neighbour in (west, east):
@@ -83,10 +96,8 @@
         pltpu.make_async_copy(gain_two_hbm, gain_two_ref, load_sem.at[7]),
         pltpu.make_async_copy(bias_hbm, bias_ref, load_sem.at[8]),
     ]
-    for at in (0, 5, 6, 7, 8, 1):
+    for at in (8, 0, 5, 6, 7, 1, 2, 3, 4):
         loads[at].start()
-    pl.semaphore_wait(barrier, 2)
-    near = 4
     spans = (
         (east, columns - near, reach - near, near),
         (west, 0, reach + columns, near),
@@ -104,10 +115,32 @@
         )
         for at, (who, source, target, size) in enumerate(spans)
     ]
-    for send in sends:
-        send.start()
-    for at in (2, 3, 4):
-        loads[at].start()
+    first = me == 0
+    second = jnp.logical_and(core == 1, me != axis - 1)
+
+    def exchange(now):
+        @pl.when(now)
+        def _():
+            pl.semaphore_wait(barrier, 2)
+            for send in sends:
+                send.start()
+
+    exchange(jnp.logical_not(jnp.logical_or(first, second)))
+
+    def arrive(far, side):
+        start = side * (columns + reach + (0 if not far else near)) + (1 - side) * (
+            0 if far else reach - near
+        )
+        size = reach - near if far else near
+        pltpu.make_async_remote_copy(
+            src_ref=tok_ref.at[0:size],
+            dst_ref=wide.at[pl.ds(start, size)],
+            send_sem=send_sem.at[2 * far + side],
+            recv_sem=recv_sem.at[2 * far + side],
+            device_id={"lon": east},
+            device_id_type=pl.DeviceIdType.MESH,
+        ).wait_recv()
+
     offsets = 2 * window - 1
     loads[8].wait()
     row = lax.broadcasted_iota(jnp.int32, (128, 128), 0)
@@ -139,13 +172,13 @@
                 jnp.where(valid, rolled, MASKED)
             )
 
+    exchange(second)
     rows = lax.broadcasted_iota(jnp.int32, (lat, width), 0)
 
     def mix(first, count):
         gain_one = gain_one_ref[...]
-
-        def column(index, carry):
-            j = first + index
+        for m in range(first, first + count):
+            j = m + odd * (keys - 1 - 2 * m)
             x = [wide[j + p].astype(F32) for p in range(3)]
             y = [
                 conv_ref[0, q : q + 1] * x[0]
@@ -158,13 +191,11 @@
             total = ((x[1] + y[1]) + (above + below)).astype(BF16)
             mixed[j] = total
             normed[j] = norm(total.astype(F32), gain_one)
-            return carry
-
-        lax.fori_loop(0, count, column, 0, unroll=True)
-
-    def project(first, count):
-        flat = normed[first : first + count].reshape(count * lat, width)
-        at = slice(first * lat, (first + count) * lat)
+
+    def project(m):
+        g = m + odd * (groups - 1 - 2 * m)
+        flat = normed[pl.ds(g * tile, tile)].reshape(128, width)
+        at = pl.ds(pl.multiple_of(g * 128, 128), 128)
         k_s[at] = jnp.dot(
             flat, w_qkv[:, width : 2 * width], preferred_element_type=F32
         ).astype(BF16)
@@ -172,86 +203,116 @@
             w_vt[...], flat, (((1,), (1,)), ((), ())), preferred_element_type=F32
         ).astype(BF16)
 
+    scale = 1.0 / float(head) ** 0.5
+
+    def tile_of(late):
+        return odd if late else 1 - odd
+
+    def query(late):
+        first = radius + tile_of(late) * tile
+        q_t[late] = (
+            lax.dot_general(
+                w_qt[...],
+                normed[pl.ds(first, tile)].reshape(128, width),
+                (((1,), (1,)), ((), ())),
+                preferred_element_type=F32,
+            ).astype(BF16)
+            * scale
+        ).astype(BF16)
+
+    blank = jnp.zeros((head, 128), BF16)
+    early = span - 128
+
+    def place(block):
+        late, part, pair = block
+        size = 128 if part else early
+        off = odd * early if part else (1 - odd) * 128
+        there = pl.ds(pl.multiple_of(tile_of(late) * 128 + off, 128), size)
+        return size, pl.ds(pl.multiple_of(off, 128), size), there, slice(pair * 2 * head, (pair + 1) * 2 * head)
+
+    def score(step, block):
+        late, part, pair = block
+        size, off, there, at = place(block)
+        q_a = q_t[late, pair * 2 * head : pair * 2 * head + head]
+        q_b = q_t[late, pair * 2 * head + head : (pair + 1) * 2 * head]
+        q_two = jnp.concatenate(
+            [jnp.concatenate([q_a, blank], axis=1), jnp.concatenate([blank, q_b], axis=1)],
+            axis=0,
+        )
+        scores = jnp.dot(k_s[there, at], q_two, preferred_element_type=F32) + bias_s[pair, off]
+        score_s[step % 2, :size] = scores
+        top = jnp.max(scores, axis=0, keepdims=True)
+        if part:
+            top = jnp.maximum(top, top_s[late, pair])
+        else:
+            top_s[late, pair] = top
+        return top
+
+    def soften(step, block, top):
+        size = place(block)[0]
+        expo = jnp.exp(score_s[step % 2, :size] - top)
+        prob_s[step % 2, :size] = expo.astype(BF16)
+        return jnp.sum(expo, axis=0, keepdims=True)
+
+    def gather(step, block, top, total):
+        late, part, pair = block
+        size, _, there, at = place(block)
+        o = jnp.dot(v_t[at, there], prob_s[step % 2, :size], preferred_element_type=F32)
+        o_a, o_b = o[:head, :128], o[head:, 128:]
+        if part:
+            keep = jnp.exp(top_s[late, pair] - top)
+            scaled = 1.0 / (total + keep * sum_s[late, pair])
+            keep = keep * scaled
+            o_a = o_a * scaled[:, :128] + held[late, pair, :head] * keep[:, :128]
+            o_b = o_b * scaled[:, 128:] + held[late, pair, head:] * keep[:, 128:]
+            att_t[tile_of(late), at] = jnp.concatenate([o_a, o_b], axis=0).astype(BF16)
+        else:
+            sum_s[late, pair] = total
+            held[late, pair] = jnp.concatenate([o_a, o_b], axis=0)
+
+    def attend(blocks):
+        tops, sums = {}, {}
+        for step in range(len(blocks) + 2):
+            if step < len(blocks):
+                tops[step] = score(step, blocks[step])
+            if 0 <= step - 1 < len(blocks):
+                sums[step - 1] = soften(step - 1, blocks[step - 1], tops[step - 1])
+            if 0 <= step - 2 < len(blocks):
+                gather(step - 2, blocks[step - 2], tops[step - 2], sums[step - 2])
+
     for at in (0, 5, 6, 7):
         loads[at].wait()
     mix(reach, columns - 2)
     loads[1].wait()
     w_qt[...] = w_qkv[:, :width].T
     w_vt[...] = w_qkv[:, 2 * width : 3 * width].T
-    west_end = -(-reach // tile) * tile
-    east_start = (keys - reach) // tile * tile
-    project(west_end, east_start - west_end)
-    sends[0].wait_recv()
-    sends[1].wait_recv()
-    mix(reach - near, near)
-    mix(reach + columns - 2, near)
-    scale = 1.0 / float(head) ** 0.5
-    q_t[...] = (
-        lax.dot_general(
-            w_qt[...],
-            normed[radius : radius + columns].reshape(columns * lat, width),
-            (((1,), (1,)), ((), ())),
-            preferred_element_type=F32,
-        ).astype(BF16)
-        * scale
-    ).astype(BF16)
-    project(west_end // 2, west_end // 2)
-    project(east_start, tile)
+    project(2)
+    exchange(first)
+    arrive(0, 1 - odd)
+    mix(keys - reach, near)
+    project(3)
+    query(0)
+    arrive(1, 1 - odd)
+    mix(keys - tile, tile)
+    project(4)
+    attend([(0, 0, pair) for pair in range(pairs)])
+    arrive(0, odd)
+    mix(tile, near)
+    query(1)
+    project(1)
+    attend([(0, 1, pair) for pair in range(pairs)] + [(1, 0, pair) for pair in range(pairs)])
     for at in (2, 3, 4):
         loads[at].wait()
-    sends[2].wait_recv()
-    sends[3].wait_recv()
-    mix(0, reach - near)
-    project(0, west_end // 2)
-    mix(reach + columns - 2 + near, reach - near)
-    project(east_start + tile, keys - east_start - tile)
-    blank = jnp.zeros((head, 128), BF16)
-
-    def place(block):
-        t, pair = divmod(block, pairs)
-        here = slice(t * 128, (t + 1) * 128)
-        there = slice(t * 128, t * 128 + span)
-        return here, there, pair, slice(pair * 2 * head, (pair + 1) * 2 * head)
-
-    def score(block):
-        here, there, pair, at = place(block)
-        q_a = q_t[pair * 2 * head : pair * 2 * head + head, here]
-        q_b = q_t[pair * 2 * head + head : (pair + 1) * 2 * head, here]
-        q_two = jnp.concatenate(
-            [jnp.concatenate([q_a, blank], axis=1), jnp.concatenate([blank, q_b], axis=1)],
-            axis=0,
-        )
-        scores = jnp.dot(k_s[there, at], q_two, preferred_element_type=F32) + bias_s[pair]
-        score_s[block % 2] = scores
-        return jnp.max(scores, axis=0, keepdims=True)
-
-    def soften(block, top):
-        expo = jnp.exp(score_s[block % 2] - top)
-        prob_s[block % 2] = expo.astype(BF16)
-        return jnp.sum(expo, axis=0, keepdims=True)
-
-    def gather(block, denom):
-        here, there, pair, at = place(block)
-        o = jnp.dot(v_t[at, there], prob_s[block % 2], preferred_element_type=F32)
-        o = jnp.concatenate(
-            [o[:head, :128] / denom[:, :128], o[head:, 128:] / denom[:, 128:]], axis=0
-        )
-        att_t[at, here] = o.astype(BF16)
-
-    blocks = columns // tile * pairs
-    tops, sums = {}, {}
-    for step in range(blocks + 2):
-        if step < blocks:
-            tops[step] = score(step)
-        if 0 <= step - 1 < blocks:
-            sums[step - 1] = soften(step - 1, tops[step - 1])
-        if 0 <= step - 2 < blocks:
-            gather(step - 2, sums[step - 2])
+    arrive(1, odd)
+    mix(0, tile)
+    project(0)
+    attend([(1, 1, pair) for pair in range(pairs)])
 
     flat_in = mixed[radius : radius + columns].reshape(columns * lat, width)
+    attended = jnp.concatenate([att_t[t] for t in range(columns // tile)], axis=1)
     stream = (
         flat_in.astype(F32) + lax.dot_general(
-            att_t[...], w_out[...], (((0,), (0,)), ((), ())), preferred_element_type=F32
+            attended, w_out[...], (((0,), (0,)), ((), ())), preferred_element_type=F32
         )
     ).astype(BF16)
     normed_two = norm(stream.astype(F32), gain_two_ref[...])
@@ -266,7 +327,7 @@
         now = ahead
         if at + chunk < ff:
             ahead = raise_(at + chunk)
-        hidden = jax.nn.gelu(now).astype(BF16)
+        hidden = gelu(now.astype(BF16))
         total = total + jnp.dot(hidden, w_down[at : at + chunk], preferred_element_type=F32)
     out_ref[...] = total.astype(BF16).reshape(columns, lat, width)
     for send in sends:
@@ -280,7 +341,6 @@
     radius = (window - 1) // 2
     keys = columns + 2 * radius
     dims = (columns, lat, width, heads, window, ff)
-    rows = columns * lat
     vmem = pl.BlockSpec(memory_space=pltpu.VMEM)
     hbm = pl.BlockSpec(memory_space=pltpu.MemorySpace.HBM)
     return pl.pallas_call(
@@ -292,15 +352,18 @@
             pltpu.VMEM((keys + 2, lat, width), BF16),
             pltpu.VMEM((keys, lat, width), BF16),
             pltpu.VMEM((keys, lat, width), BF16),
-            pltpu.VMEM((width, rows), BF16),
+            pltpu.VMEM((2, width, 128), BF16),
             pltpu.VMEM((keys * lat, width), BF16),
             pltpu.VMEM((width, keys * lat), BF16),
-            pltpu.VMEM((width, rows), BF16),
+            pltpu.VMEM((2, width, 128), BF16),
             pltpu.VMEM((heads // 2, keys * lat - 128, 256), F32),
             pltpu.VMEM((width, width), BF16),
             pltpu.VMEM((width, width), BF16),
             pltpu.VMEM((2, keys * lat - 128, 256), F32),
             pltpu.VMEM((2, keys * lat - 128, 256), BF16),
+            pltpu.VMEM((2, heads // 2, 1, 256), F32),
+            pltpu.VMEM((2, heads // 2, 1, 256), F32),
+            pltpu.VMEM((2, heads // 2, 2 * width // heads, 128), F32),
             pltpu.VMEM(w_qkv.shape, BF16),
             pltpu.VMEM(w_out.shape, BF16),
             pltpu.VMEM(w_up.shape, BF16),

time: 15.8 us -> 14.5 us (0.918)
  Pallas kernels: 14.9 us -> 13.7 us
    pallas_call x1, Pallas kernels: 14.9 us -> 13.7 us  [on_device(): pl.pallas_call(functools.partial(block_kernel, dims), out_shape=pltpu.VME...]
where the time goes in v1:
time: 14.5 us; the launch traced here: 14.4 us
  Pallas kernels  13.7 us (94%)
  local copies, waits for them, and re-layouts  0.71 us (5%)
    pallas_call x1, Pallas kernels, on_device(): pl.pallas_call(functools.partial(block_kernel, dims), out_shape=pltpu.VME...  13.7 us
    unnamed x1, local copies, waits for them, and re-layouts  0.71 us

profile of v1, /device:TPU:0, one launch (start us, length us, event | category | flops | bytes accessed | tf_op | source)
XLA Modules:
  0.0 14.4 jit_solution(10376823272699198604)
XLA Ops:
  0.0 13.7 %shard_map.91 = bf16[8,32,512]{2,1,0:T(8,128)(2,1)S(1)} custom-call(bf16[8,32,512]{2,1,0:T(8,128)(2,1)} %tok_ref.1, f32[3,3,512]{2,1,0:T(4,128)} %conv_hbm.1, f32[1,512]{1,0:T(1,128)} %bitcast.4, f32[1,512]{1,0:T(1,128)} %bitcast.5, bf16[512,1536]{1,0:T(8,128)(2,1)} %w_qkv_ref.1, f32[13,8,25]{2,1,0:T(8,128)} %bitcast.3, bf16[512,512]{1,0:T(8,128)(2,1)} %w_out_ref.1, ...), custom_call_target="tpu_custom_call" | custom-call | tf_op jit(solution)/shard_map/pallas_call | solution.py:346
  13.7 0.7 %copy.11 = bf16[8,32,512]{2,1,0:T(8,128)(2,1)} copy(bf16[8,32,512]{2,1,0:T(8,128)(2,1)S(1)} %shard_map.91) | data formatting | bytes 524288

commit v2 on v1

--- a/solution.py
+++ b/solution.py
@@ -8,6 +8,7 @@
 from jax.sharding import PartitionSpec as P
 
 EPS = 1e-05
+LOG2E = 1.4426950408889634
 F32 = jnp.float32
 BF16 = jnp.bfloat16
 MASKED = -1e30
@@ -153,6 +154,7 @@
             jnp.dot(
                 piece, flip, preferred_element_type=F32, precision=lax.Precision.HIGHEST
             )
+            * LOG2E
         )
     key_row = lax.broadcasted_iota(jnp.int32, (lat, 128), 0)
     lane = lax.broadcasted_iota(jnp.int32, (lat, 128), 1)
@@ -177,18 +179,27 @@
 
     def mix(first, count):
         gain_one = gain_one_ref[...]
+        taps = [conv_ref[r + odd * (2 - 2 * r)] for r in range(3)]
+        taps[1] = taps[1] + (lax.broadcasted_iota(jnp.int32, (3, width), 0) == 1).astype(F32)
+
+        def fetch(u):
+            return wide[u + odd * (keys + 1 - 2 * u)].astype(F32)
+
+        x = [fetch(first), fetch(first + 1)]
         for m in range(first, first + count):
             j = m + odd * (keys - 1 - 2 * m)
-            x = [wide[j + p].astype(F32) for p in range(3)]
+            x = x[-2:] + [fetch(m + 2)]
             y = [
-                conv_ref[0, q : q + 1] * x[0]
-                + conv_ref[1, q : q + 1] * x[1]
-                + conv_ref[2, q : q + 1] * x[2]
+                taps[0][q : q + 1] * x[0] + taps[1][q : q + 1] * x[1] + taps[2][q : q + 1] * x[2]
                 for q in range(3)
             ]
-            above = jnp.where(rows == 0, 0.0, pltpu.roll(y[0], 1, 0))
-            below = jnp.where(rows == lat - 1, 0.0, pltpu.roll(y[2], lat - 1, 0))
-            total = ((x[1] + y[1]) + (above + below)).astype(BF16)
+            above = pltpu.roll(y[0], 1, 0)
+            above = jnp.concatenate([jnp.where(rows[:8] == 0, 0.0, above[:8]), above[8:]], axis=0)
+            below = pltpu.roll(y[2], lat - 1, 0)
+            below = jnp.concatenate(
+                [below[: lat - 8], jnp.where(rows[lat - 8 :] == lat - 1, 0.0, below[lat - 8 :])], axis=0
+            )
+            total = (y[1] + (above + below)).astype(BF16)
             mixed[j] = total
             normed[j] = norm(total.astype(F32), gain_one)
 
@@ -203,7 +214,7 @@
             w_vt[...], flat, (((1,), (1,)), ((), ())), preferred_element_type=F32
         ).astype(BF16)
 
-    scale = 1.0 / float(head) ** 0.5
+    scale = LOG2E / float(head) ** 0.5
 
     def tile_of(late):
         return odd if late else 1 - odd
@@ -216,7 +227,7 @@
                 normed[pl.ds(first, tile)].reshape(128, width),
                 (((1,), (1,)), ((), ())),
                 preferred_element_type=F32,
-            ).astype(BF16)
+            )
             * scale
         ).astype(BF16)
 
@@ -250,17 +261,18 @@
 
     def soften(step, block, top):
         size = place(block)[0]
-        expo = jnp.exp(score_s[step % 2, :size] - top)
-        prob_s[step % 2, :size] = expo.astype(BF16)
-        return jnp.sum(expo, axis=0, keepdims=True)
-
-    def gather(step, block, top, total):
+        prob_s[step % 2, :size] = jnp.exp2((score_s[step % 2, :size] - top).astype(BF16))
+
+    def gather(step, block, top):
         late, part, pair = block
         size, _, there, at = place(block)
         o = jnp.dot(v_t[at, there], prob_s[step % 2, :size], preferred_element_type=F32)
+        total = jnp.dot(
+            jnp.ones((16, size), BF16), prob_s[step % 2, :size], preferred_element_type=F32
+        )[:1]
         o_a, o_b = o[:head, :128], o[head:, 128:]
         if part:
-            keep = jnp.exp(top_s[late, pair] - top)
+            keep = jnp.exp2(top_s[late, pair] - top)
             scaled = 1.0 / (total + keep * sum_s[late, pair])
             keep = keep * scaled
             o_a = o_a * scaled[:, :128] + held[late, pair, :head] * keep[:, :128]
@@ -271,14 +283,14 @@
             held[late, pair] = jnp.concatenate([o_a, o_b], axis=0)
 
     def attend(blocks):
-        tops, sums = {}, {}
+        tops = {}
         for step in range(len(blocks) + 2):
             if step < len(blocks):
                 tops[step] = score(step, blocks[step])
             if 0 <= step - 1 < len(blocks):
-                sums[step - 1] = soften(step - 1, blocks[step - 1], tops[step - 1])
+                soften(step - 1, blocks[step - 1], tops[step - 1])
             if 0 <= step - 2 < len(blocks):
-                gather(step - 2, blocks[step - 2], tops[step - 2], sums[step - 2])
+                gather(step - 2, blocks[step - 2], tops[step - 2])
 
     for at in (0, 5, 6, 7):
         loads[at].wait()
@@ -287,11 +299,11 @@
     w_qt[...] = w_qkv[:, :width].T
     w_vt[...] = w_qkv[:, 2 * width : 3 * width].T
     project(2)
-    exchange(first)
     arrive(0, 1 - odd)
     mix(keys - reach, near)
     project(3)
     query(0)
+    exchange(first)
     arrive(1, 1 - odd)
     mix(keys - tile, tile)
     project(4)

time: 14.5 us -> 14.3 us (0.986)
  Pallas kernels: 13.7 us -> 13.5 us
    pallas_call x1, Pallas kernels: 13.7 us -> 13.5 us  [on_device(): pl.pallas_call(functools.partial(block_kernel, dims), out_shape=pltpu.VME...]
where the time goes in v2:
time: 14.3 us; the launch traced here: 14.2 us
  Pallas kernels  13.5 us (94%)
  local copies, waits for them, and re-layouts  0.71 us (5%)
    pallas_call x1, Pallas kernels, on_device(): pl.pallas_call(functools.partial(block_kernel, dims), out_shape=pltpu.VME...  13.5 us
    unnamed x1, local copies, waits for them, and re-layouts  0.71 us

profile of v2, /device:TPU:0, one launch (start us, length us, event | category | flops | bytes accessed | tf_op | source)
XLA Modules:
  0.0 14.2 jit_solution(9899898435181232206)
XLA Ops:
  0.0 13.5 %shard_map.91 = bf16[8,32,512]{2,1,0:T(8,128)(2,1)S(1)} custom-call(bf16[8,32,512]{2,1,0:T(8,128)(2,1)} %tok_ref.1, f32[3,3,512]{2,1,0:T(4,128)} %conv_hbm.1, f32[1,512]{1,0:T(1,128)} %bitcast.4, f32[1,512]{1,0:T(1,128)} %bitcast.5, bf16[512,1536]{1,0:T(8,128)(2,1)} %w_qkv_ref.1, f32[13,8,25]{2,1,0:T(8,128)} %bitcast.3, bf16[512,512]{1,0:T(8,128)(2,1)} %w_out_ref.1, ...), custom_call_target="tpu_custom_call" | custom-call | tf_op jit(solution)/shard_map/pallas_call | solution.py:358
  13.5 0.7 %copy.11 = bf16[8,32,512]{2,1,0:T(8,128)(2,1)} copy(bf16[8,32,512]{2,1,0:T(8,128)(2,1)S(1)} %shard_map.91) | data formatting | bytes 524288

commit v3 on v2

--- a/solution.py
+++ b/solution.py
@@ -233,6 +233,7 @@
 
     blank = jnp.zeros((head, 128), BF16)
     early = span - 128
+    slots = 8
 
     def place(block):
         late, part, pair = block
@@ -251,7 +252,7 @@
             axis=0,
         )
         scores = jnp.dot(k_s[there, at], q_two, preferred_element_type=F32) + bias_s[pair, off]
-        score_s[step % 2, :size] = scores
+        score_s[step % slots, :size] = scores
         top = jnp.max(scores, axis=0, keepdims=True)
         if part:
             top = jnp.maximum(top, top_s[late, pair])
@@ -261,14 +262,14 @@
 
     def soften(step, block, top):
         size = place(block)[0]
-        prob_s[step % 2, :size] = jnp.exp2((score_s[step % 2, :size] - top).astype(BF16))
+        prob_s[step % slots, :size] = jnp.exp2((score_s[step % slots, :size] - top).astype(BF16))
 
     def gather(step, block, top):
         late, part, pair = block
         size, _, there, at = place(block)
-        o = jnp.dot(v_t[at, there], prob_s[step % 2, :size], preferred_element_type=F32)
+        o = jnp.dot(v_t[at, there], prob_s[step % slots, :size], preferred_element_type=F32)
         total = jnp.dot(
-            jnp.ones((16, size), BF16), prob_s[step % 2, :size], preferred_element_type=F32
+            jnp.ones((16, size), BF16), prob_s[step % slots, :size], preferred_element_type=F32
         )[:1]
         o_a, o_b = o[:head, :128], o[head:, 128:]
         if part:
@@ -282,15 +283,17 @@
             sum_s[late, pair] = total
             held[late, pair] = jnp.concatenate([o_a, o_b], axis=0)
 
-    def attend(blocks):
+    def attend(blocks, apart=3):
         tops = {}
-        for step in range(len(blocks) + 2):
+        for step in range(len(blocks) + 2 * apart):
             if step < len(blocks):
                 tops[step] = score(step, blocks[step])
-            if 0 <= step - 1 < len(blocks):
-                soften(step - 1, blocks[step - 1], tops[step - 1])
-            if 0 <= step - 2 < len(blocks):
-                gather(step - 2, blocks[step - 2], tops[step - 2])
+            at = step - apart
+            if 0 <= at < len(blocks):
+                soften(at, blocks[at], tops[at])
+            at = step - 2 * apart
+            if 0 <= at < len(blocks):
+                gather(at, blocks[at], tops[at])
 
     for at in (0, 5, 6, 7):
         loads[at].wait()
@@ -329,7 +332,7 @@
     ).astype(BF16)
     normed_two = norm(stream.astype(F32), gain_two_ref[...])
     total = stream.astype(F32)
-    chunk = 512
+    chunk = 1024
 
     def raise_(at):
         return jnp.dot(normed_two, w_up[:, at : at + chunk], preferred_element_type=F32)
@@ -371,8 +374,8 @@
             pltpu.VMEM((heads // 2, keys * lat - 128, 256), F32),
             pltpu.VMEM((width, width), BF16),
             pltpu.VMEM((width, width), BF16),
-            pltpu.VMEM((2, keys * lat - 128, 256), F32),
-            pltpu.VMEM((2, keys * lat - 128, 256), BF16),
+            pltpu.VMEM((8, keys * lat - 256, 256), F32),
+            pltpu.VMEM((8, keys * lat - 256, 256), BF16),
             pltpu.VMEM((2, heads // 2, 1, 256), F32),
             pltpu.VMEM((2, heads // 2, 1, 256), F32),
             pltpu.VMEM((2, heads // 2, 2 * width // heads, 128), F32),

time: 14.3 us -> 14 us (0.979)
  Pallas kernels: 13.5 us -> 13.1 us
    pallas_call x1, Pallas kernels: 13.5 us -> 13.1 us  [on_device(): pl.pallas_call(functools.partial(block_kernel, dims), out_shape=pltpu.VME...]
where the time goes in v3:
time: 14 us; the launch traced here: 13.9 us
  Pallas kernels  13.1 us (94%)
  local copies, waits for them, and re-layouts  0.71 us (5%)
    pallas_call x1, Pallas kernels, on_device(): pl.pallas_call(functools.partial(block_kernel, dims), out_shape=pltpu.VME...  13.1 us
    unnamed x1, local copies, waits for them, and re-layouts  0.71 us

profile of v3, /device:TPU:0, one launch (start us, length us, event | category | flops | bytes accessed | tf_op | source)
XLA Modules:
  0.0 13.9 jit_solution(6202811629509400879)
XLA Ops:
  0.0 13.1 %shard_map.91 = bf16[8,32,512]{2,1,0:T(8,128)(2,1)S(1)} custom-call(bf16[8,32,512]{2,1,0:T(8,128)(2,1)} %tok_ref.1, f32[3,3,512]{2,1,0:T(4,128)} %conv_hbm.1, f32[1,512]{1,0:T(1,128)} %bitcast.4, f32[1,512]{1,0:T(1,128)} %bitcast.5, bf16[512,1536]{1,0:T(8,128)(2,1)} %w_qkv_ref.1, f32[13,8,25]{2,1,0:T(8,128)} %bitcast.3, bf16[512,512]{1,0:T(8,128)(2,1)} %w_out_ref.1, ...), custom_call_target="tpu_custom_call" | custom-call | tf_op jit(solution)/shard_map/pallas_call | solution.py:361
  13.2 0.7 %copy.11 = bf16[8,32,512]{2,1,0:T(8,128)(2,1)} copy(bf16[8,32,512]{2,1,0:T(8,128)(2,1)S(1)} %shard_map.91) | data formatting | bytes 524288

commit v4 on v3

--- a/solution.py
+++ b/solution.py
@@ -47,7 +47,6 @@
     att_t,
     bias_s,
     w_qt,
-    w_vt,
     score_s,
     prob_s,
     top_s,
@@ -210,9 +209,9 @@
         k_s[at] = jnp.dot(
             flat, w_qkv[:, width : 2 * width], preferred_element_type=F32
         ).astype(BF16)
-        v_t[:, at] = lax.dot_general(
-            w_vt[...], flat, (((1,), (1,)), ((), ())), preferred_element_type=F32
-        ).astype(BF16)
+        v_t[:, at] = jnp.dot(
+            flat, w_qkv[:, 2 * width : 3 * width], preferred_element_type=F32
+        ).astype(BF16).T
 
     scale = LOG2E / float(head) ** 0.5
 
@@ -300,7 +299,6 @@
     mix(reach, columns - 2)
     loads[1].wait()
     w_qt[...] = w_qkv[:, :width].T
-    w_vt[...] = w_qkv[:, 2 * width : 3 * width].T
     project(2)
     arrive(0, 1 - odd)
     mix(keys - reach, near)
@@ -372,7 +370,6 @@
             pltpu.VMEM((width, keys * lat), BF16),
             pltpu.VMEM((2, width, 128), BF16),
             pltpu.VMEM((heads // 2, keys * lat - 128, 256), F32),
-            pltpu.VMEM((width, width), BF16),
             pltpu.VMEM((width, width), BF16),
             pltpu.VMEM((8, keys * lat - 256, 256), F32),
             pltpu.VMEM((8, keys * lat - 256, 256), BF16),

time: 14 us -> 13.8 us (0.986)
  Pallas kernels: 13.1 us -> 12.9 us
    pallas_call x1, Pallas kernels: 13.1 us -> 12.9 us  [on_device(): pl.pallas_call(functools.partial(block_kernel, dims), out_shape=pltpu.VME...]
where the time goes in v4:
time: 13.8 us; the launch traced here: 13.7 us
  Pallas kernels  12.9 us (93%)
  local copies, waits for them, and re-layouts  0.71 us (5%)
    pallas_call x1, Pallas kernels, on_device(): pl.pallas_call(functools.partial(block_kernel, dims), out_shape=pltpu.VME...  12.9 us
    unnamed x1, local copies, waits for them, and re-layouts  0.71 us

profile of v4, /device:TPU:0, one launch (start us, length us, event | category | flops | bytes accessed | tf_op | source)
XLA Modules:
  0.0 13.7 jit_solution(10061974058388928208)
XLA Ops:
  0.0 12.9 %shard_map.91 = bf16[8,32,512]{2,1,0:T(8,128)(2,1)S(1)} custom-call(bf16[8,32,512]{2,1,0:T(8,128)(2,1)} %tok_ref.1, f32[3,3,512]{2,1,0:T(4,128)} %conv_hbm.1, f32[1,512]{1,0:T(1,128)} %bitcast.4, f32[1,512]{1,0:T(1,128)} %bitcast.5, bf16[512,1536]{1,0:T(8,128)(2,1)} %w_qkv_ref.1, f32[13,8,25]{2,1,0:T(8,128)} %bitcast.3, bf16[512,512]{1,0:T(8,128)(2,1)} %w_out_ref.1, ...), custom_call_target="tpu_custom_call" | custom-call | tf_op jit(solution)/shard_map/pallas_call | solution.py:359
  13.0 0.7 %copy.11 = bf16[8,32,512]{2,1,0:T(8,128)(2,1)} copy(bf16[8,32,512]{2,1,0:T(8,128)(2,1)S(1)} %shard_map.91) | data formatting | bytes 524288
